TPU v7x, 256 devices: a whole 4x4x8 slice. The times are simulated.
256 devices in a mesh: dp: 16 (over z_hi, y), tensor: 16 (over x, z_lo, core).
Axes of the slice: x: 4, y: 4, z: 8 (z_hi: 4, z_lo: 2; z = z_hi * 2 + z_lo), core: 2. Of those that a mesh axis runs over, the one named last changes fastest.
Arguments:
- tokens: bfloat16 [12288, 8192], P('dp', 'tensor'), may hold values from -6 to 6
- r_up: bfloat16 [16, 512, 1024], P('tensor', 'dp'), may hold values from -0.25 to 0.25
- l_up: bfloat16 [16, 1024, 1024], P('tensor', 'dp'), may hold values from -0.1875 to 0.1875
- r_down: bfloat16 [16, 1024, 1024], P('tensor', 'dp'), may hold values from -0.1875 to 0.1875
- l_down: bfloat16 [16, 1024, 512], P('tensor', 'dp'), may hold values from -0.1875 to 0.1875
- mask_r_up: int32 [16, 4, 8], P('tensor'), may hold values 0 or 1
- mask_l_up: int32 [16, 8, 8], P('tensor'), may hold values 0 or 1
- mask_r_down: int32 [16, 8, 8], P('tensor'), may hold values 0 or 1
- mask_l_down: int32 [16, 8, 4], P('tensor'), may hold values 0 or 1
- cotangent: bfloat16 [12288, 8192], P('dp', 'tensor'), may hold values from -6 to 6
Outputs:
- mixed: bfloat16 [12288, 8192], P('dp', 'tensor')
- tokens_grad: bfloat16 [12288, 8192], P('dp', 'tensor')
- r_up_grad: float32 [16, 512, 1024], P('tensor', 'dp')
- l_up_grad: float32 [16, 1024, 1024], P('tensor', 'dp')
- r_down_grad: float32 [16, 1024, 1024], P('tensor', 'dp')
- l_down_grad: float32 [16, 1024, 512], P('tensor', 'dp')
Inputs may be any that keep to these rules, and one draw needn't show every extreme that they name: `mask_r_up`: 1 keeps a 128 x 128 tile of a factor's block, 0 drops it. `mask_l_up`: 1 keeps a 128 x 128 tile of a factor's block, 0 drops it. `mask_r_down`: 1 keeps a 128 x 128 tile of a factor's block, 0 drops it. `mask_l_down`: 1 keeps a 128 x 128 tile of a factor's block, 0 drops it.
All inputs are finite; a program needn't handle non-finite values.
Results may differ from a plain program's by a relative error of at most 0.018.
Values may be sent and summed in bfloat16 or wider, within the bound.
A program may use at most 128 MiB of HBM per device.

v0:
```python
import math

import jax
import jax.numpy as jnp
from jax import lax
from jax.sharding import PartitionSpec as P


def spread(mask, rows, cols):
    table = mask[0].astype(jnp.float32)
    row_tiles, col_tiles = table.shape
    full = jnp.broadcast_to(
        table[:, None, :, None], (row_tiles, rows // row_tiles, col_tiles, cols // col_tiles)
    )
    return full.reshape(rows, cols)


def masked(weight, mask):
    rows, cols = (weight.shape[1], weight.shape[2])
    return weight[0] * spread(mask, rows, cols).astype(jnp.bfloat16)


def mult_back(left, weight):
    return lax.dot_general(
        left, weight, (((1,), (1,)), ((), ())), preferred_element_type=jnp.float32
    )


def gelu_tanh(value):
    return jax.nn.gelu(value, approximate=True)


def make_term(left, right, mask_full, scale):

    def term(start, count):
        part = lax.dot_general(
            left, right, (((0,), (0,)), ((), ())), preferred_element_type=jnp.float32
        )
        return part * scale * mask_full

    return term


def per_device(
    tokens, r_up, l_up, r_down, l_down, mask_r_up, mask_l_up, mask_r_down, mask_l_down, cotangent
):
    factors = (
        lax.all_gather(r_up, "dp", axis=1, tiled=True),
        lax.all_gather(l_up, "dp", axis=1, tiled=True),
        lax.all_gather(r_down, "dp", axis=1, tiled=True),
        lax.all_gather(l_down, "dp", axis=1, tiled=True),
    )
    w_r_up = masked(factors[0], mask_r_up)
    w_l_up = masked(factors[1], mask_l_up)
    w_r_down = masked(factors[2], mask_r_down)
    w_l_down = masked(factors[3], mask_l_down)
    first = jnp.dot(tokens, w_r_up, preferred_element_type=jnp.float32).astype(jnp.bfloat16)
    piece = lax.all_to_all(first, "tensor", split_axis=1, concat_axis=1, tiled=True)
    moved = piece
    inner = jnp.dot(piece, w_l_up, preferred_element_type=jnp.float32)
    active = gelu_tanh(inner).astype(jnp.bfloat16)
    lowered = jnp.dot(active, w_r_down, preferred_element_type=jnp.float32).astype(jnp.bfloat16)
    piece = lax.all_to_all(lowered, "tensor", split_axis=1, concat_axis=1, tiled=True)
    mixed = jnp.dot(piece, w_l_down, preferred_element_type=jnp.float32).astype(jnp.bfloat16)
    scale = 1.0 / math.sqrt(tokens.shape[0] * lax.axis_size("dp"))
    width = tokens.shape[1]
    hidden = first.shape[1]
    full_r_up = spread(mask_r_up, width, hidden)
    full_l_up = spread(mask_l_up, hidden, hidden)
    full_r_down = spread(mask_r_down, hidden, hidden)
    full_l_down = spread(mask_l_down, hidden, width)
    d_lowered_moved = mult_back(cotangent, w_l_down).astype(jnp.bfloat16)
    term_l_down = make_term(piece, cotangent, full_l_down, scale)
    d_lowered = lax.all_to_all(d_lowered_moved, "tensor", split_axis=1, concat_axis=1, tiled=True)
    d_active = mult_back(d_lowered, w_r_down)
    unused, pull = jax.vjp(gelu_tanh, inner)
    d_inner = pull(d_active)[0].astype(jnp.bfloat16)
    term_r_down = make_term(active, d_lowered, full_r_down, scale)
    d_moved = mult_back(d_inner, w_l_up).astype(jnp.bfloat16)
    term_l_up = make_term(moved, d_inner, full_l_up, scale)
    d_first = lax.all_to_all(d_moved, "tensor", split_axis=1, concat_axis=1, tiled=True)
    tokens_grad = mult_back(d_first, w_r_up).astype(jnp.bfloat16)
    term_r_up = make_term(tokens, d_first, full_r_up, scale)
    r_up_grad, l_up_grad, r_down_grad, l_down_grad = (
        lax.psum_scatter(
            term_r_up(0, width).astype(jnp.bfloat16), "dp", scatter_dimension=0, tiled=True
        ).astype(jnp.float32),
        lax.psum_scatter(
            term_l_up(0, hidden).astype(jnp.bfloat16), "dp", scatter_dimension=0, tiled=True
        ).astype(jnp.float32),
        lax.psum_scatter(
            term_r_down(0, hidden).astype(jnp.bfloat16), "dp", scatter_dimension=0, tiled=True
        ).astype(jnp.float32),
        lax.psum_scatter(
            term_l_down(0, hidden).astype(jnp.bfloat16), "dp", scatter_dimension=0, tiled=True
        ).astype(jnp.float32),
    )
    return (
        mixed,
        tokens_grad,
        r_up_grad[None],
        l_up_grad[None],
        r_down_grad[None],
        l_down_grad[None],
    )


def solution(mesh):
    return jax.shard_map(
        per_device,
        mesh=mesh,
        in_specs=(
            P("dp", "tensor"),
            P("tensor", "dp", None),
            P("tensor", "dp", None),
            P("tensor", "dp", None),
            P("tensor", "dp", None),
            P("tensor", None, None),
            P("tensor", None, None),
            P("tensor", None, None),
            P("tensor", None, None),
            P("dp", "tensor"),
        ),
        out_specs=(
            P("dp", "tensor"),
            P("dp", "tensor"),
            P("tensor", "dp", None),
            P("tensor", "dp", None),
            P("tensor", "dp", None),
            P("tensor", "dp", None),
        ),
        check_vma=False,
    )
```

profile of v0, /device:TPU:32, one launch (start us, length us, event | category | flops | bytes accessed | tf_op | source)
XLA Modules:
  0.0 615.0 jit_solution(5140028775005074)
XLA Ops:
  8.0 0.7 all-gather.11.cloned.1.call-update
  9.4 0.7 fusion.43
  10.2 54.7 %all-gather.5.cloned.1.call-done = bf16[1,512,1024]{2,1,0:T(8,128)(2,1)} async-done(((bf16[1,32,1024]{2,1,0:T(8,128)(2,1)}), bf16[1,512,1024]{2,1,0:T(8,128)(2,1)}) %all-gather.5.cloned.1.call-update) | async-done | bytes 1048592 | tf_op jit(solution)/shard_map/all_gather | solution.py:48
  64.9 1.5 copy.30
  66.7 2.2 convolution_convert_fusion.1
  68.9 7.0 %all-to-all-start = ((bf16[768,16,64]{0,2,1:T(8,128)(2,1)}), bf16[768,16,64]{0,2,1:T(8,128)(2,1)S(1)}, u32[]{:S(2)}, u32[]{:S(2)}) async-start(bf16[768,16,64]{0,2,1:T(8,128)(2,1)} %bitcast.158), calls=%async_computation | async-start | bytes 3145728 | tf_op jit(solution)/shard_map/all_to_all | solution.py:58
  76.5 42.2 %all-gather.11.cloned.1.call-done = bf16[1,1024,512]{2,1,0:T(8,128)(2,1)} async-done(((bf16[1,64,512]{2,1,0:T(8,128)(2,1)}), bf16[1,1024,512]{2,1,0:T(8,128)(2,1)}) %all-gather.11.cloned.1.call-update) | async-done | bytes 1048592 | tf_op jit(solution)/shard_map/all_gather | solution.py:51
  119.1 1.3 copy-done.9
  120.4 3.3 convolution_convert_fusion
  123.7 7.0 %all-to-all-start.2 = ((bf16[768,16,64]{0,2,1:T(8,128)(2,1)}), bf16[768,16,64]{0,2,1:T(8,128)(2,1)}, u32[]{:S(2)}, u32[]{:S(2)}) async-start(bf16[768,16,64]{0,2,1:T(8,128)(2,1)} %bitcast.157), calls=%async_computation.2 | async-start | bytes 3145728 | tf_op jit(solution)/shard_map/all_to_all | solution.py:74
  130.8 1.7 broadcast_in_dim.73
  132.4 2.8 convert_element_type.162
  135.3 1.7 broadcast_in_dim.77
  137.0 4.2 convert_element_type.177
  141.2 38.4 %all-gather.7.cloned.1.call-done = bf16[1,1024,1024]{2,1,0:T(8,128)(2,1)} async-done(((bf16[1,64,1024]{2,1,0:T(8,128)(2,1)}), bf16[1,1024,1024]{2,1,0:T(8,128)(2,1)}) %all-gather.7.cloned.1.call-update) | async-done | bytes 2097168 | tf_op jit(solution)/shard_map/all_gather | solution.py:49
  179.6 5.5 fusion.23
  185.2 54.2 %all-gather.9.cloned.1.call-done = bf16[1,1024,1024]{2,1,0:T(8,128)(2,1)} async-done(((bf16[1,64,1024]{2,1,0:T(8,128)(2,1)}), bf16[1,1024,1024]{2,1,0:T(8,128)(2,1)}) %all-gather.9.cloned.1.call-update) | async-done | bytes 2097168 | tf_op jit(solution)/shard_map/all_gather | solution.py:50
  239.3 7.2 %fusion.8 = bf16[768,1024]{1,0:T(8,128)(2,1)S(1)} fusion(f32[768,1024]{1,0:T(8,128)} %fusion.23, bf16[768,1024]{0,1:T(8,128)(2,1)} %bitcast.16, bf16[1,1024,1024]{2,1,0:T(8,128)(2,1)} %all-gather.9.cloned.1.call-done, bf16[1,1024,1024]{2,1,0:T(8,128)(2,1)} %convert_element_type.177), kind=kOutput, calls=%fused_computation.14 | convolution fusion | flops 1627389952 | bytes 10485760 | tf_op jit(solution)/shard_map/dot_general | solution.py:24
  246.9 0.8 copy-done.18
  247.7 1.4 copy-done.3
  249.2 3.5 fusion
  253.2 2.1 copy-done.4
  255.3 0.9 copy-done.5
  256.2 5.1 fusion.1
  261.3 1.6 copy-done.6
  262.9 5.8 fusion.27
  268.7 2.6 copy.35
  271.3 5.7 all-to-all-start.3
  277.0 6.2 %fusion.30 = bf16[768,1024]{1,0:T(8,128)(2,1)S(1)} fusion(f32[128,8,8,128]{3,2,1,0:T(8,128)} %bitcast.152, bf16[1,1024,1024]{2,1,0:T(8,128)(2,1)} %all-gather.9.cloned.1.call-done, f32[768,1024]{1,0:T(8,128)} %fusion.23), kind=kOutput, calls=%fused_computation.37 | convolution fusion | flops 1619525632 | bytes 11010048 | tf_op jit(solution)/shard_map/dot_general | solution.py:62
  283.2 1.6 copy.32
  284.8 20.3 %all-to-all-done.3 = bf16[768,16,64]{0,2,1:T(8,128)(2,1)} async-done(((bf16[768,16,64]{0,2,1:T(8,128)(2,1)}), bf16[768,16,64]{0,2,1:T(8,128)(2,1)}, u32[]{:S(2)}, u32[]{:S(2)}) %all-to-all-start.3) | async-done | bytes 1572896 | tf_op jit(solution)/shard_map/all_to_all | solution.py:81
  305.0 8.2 %all-to-all-start.1 = ((bf16[768,16,64]{0,2,1:T(8,128)(2,1)}), bf16[768,16,64]{0,2,1:T(8,128)(2,1)}, u32[]{:S(2)}, u32[]{:S(2)}) async-start(bf16[768,16,64]{0,2,1:T(8,128)(2,1)} %bitcast.9), calls=%async_computation.1 | async-start | bytes 3145728 | tf_op jit(solution)/shard_map/all_to_all | solution.py:63
  313.3 3.4 fusion.16
  316.7 2.4 copy.37
  319.2 16.4 %all-to-all-done.1 = bf16[768,16,64]{0,2,1:T(8,128)(2,1)} async-done(((bf16[768,16,64]{0,2,1:T(8,128)(2,1)}), bf16[768,16,64]{0,2,1:T(8,128)(2,1)}, u32[]{:S(2)}, u32[]{:S(2)}) %all-to-all-start.1) | async-done | bytes 1572896 | tf_op jit(solution)/shard_map/all_to_all | solution.py:63
  335.6 3.6 fusion.15
  339.5 1.3 convert_element_type.182
  341.2 1.2 convert_element_type.171
  342.4 3.8 convolution_convert_fusion.2
  346.2 3.3 convolution_convert_fusion.3
  349.5 1.6 bitcast_convert_fusion.6
  351.2 79.8 %reduce-scatter.9.cloned.1.call-done = bf16[64,1024]{1,0:T(8,128)(2,1)} async-done(((bf16[1024,1024]{1,0:T(8,128)(2,1)}), bf16[64,1024]{1,0:T(8,128)(2,1)}) %reduce-scatter.9.cloned.1.call-update) | async-done | bytes 131088 | tf_op jit(solution)/shard_map/reduce_scatter | solution.py:91
  430.9 1.6 bitcast_convert_fusion.5
  432.6 86.0 %reduce-scatter.13.cloned.1.call-done = bf16[32,1024]{1,0:T(8,128)(2,1)} async-done(((bf16[512,1024]{1,0:T(8,128)(2,1)}), bf16[32,1024]{1,0:T(8,128)(2,1)}) %reduce-scatter.13.cloned.1.call-update) | async-done | bytes 65552
  518.6 1.0 copy.38
  519.7 0.8 copy.36
  520.5 86.1 %reduce-scatter.11.cloned.1.call-done = bf16[64,512]{1,0:T(8,128)(2,1)} async-done(((bf16[1024,512]{1,0:T(8,128)(2,1)}), bf16[64,512]{1,0:T(8,128)(2,1)}) %reduce-scatter.11.cloned.1.call-update) | async-done | bytes 65552 | tf_op jit(solution)/shard_map/reduce_scatter | solution.py:94
  606.6 1.5 bitcast_convert_fusion.7
  (63 shorter events, 4.8 us)
Async XLA Ops:
  7.2 59.5 %copy-start = (bf16[768,512]{1,0:T(8,128)(2,1)S(1)}, bf16[768,512]{1,0:T(8,128)(2,1)}, u32[]{:S(2)}) copy-start(bf16[768,512]{1,0:T(8,128)(2,1)} %param.10) | copy-start | bytes 2359300
  7.2 57.7 %all-gather.5.cloned.1.call-start = ((), (), s32[]{:S(2)}) async-start(), calls=%async_computation.8 | async-start | bytes 1114112 | tf_op jit(solution)/shard_map/all_gather | solution.py:48
  7.9 110.8 %all-gather.11.cloned.1.call-start = ((), (), s32[]{:S(2)}) async-start(), calls=%async_computation.11 | async-start | bytes 1114112 | tf_op jit(solution)/shard_map/all_gather | solution.py:51
  8.7 171.0 %all-gather.7.cloned.1.call-start = ((), (), s32[]{:S(2)}) async-start(), calls=%async_computation.9 | async-start | bytes 2228224 | tf_op jit(solution)/shard_map/all_gather | solution.py:49
  66.7 2.2 copy-start.7
  68.9 7.5 %copy-start.15 = (s32[1,8,4]{1,2,0:T(4,128)S(1)}, s32[1,8,4]{1,2,0:T(4,128)}, u32[]{:S(2)}) copy-start(s32[1,8,4]{1,2,0:T(4,128)} %param.18) | copy-start | bytes 388
  68.9 54.8 %all-to-all-start = ((bf16[768,16,64]{0,2,1:T(8,128)(2,1)}), bf16[768,16,64]{0,2,1:T(8,128)(2,1)S(1)}, u32[]{:S(2)}, u32[]{:S(2)}) async-start(bf16[768,16,64]{0,2,1:T(8,128)(2,1)} %bitcast.158), calls=%async_computation | async-start | bytes 3145728 | tf_op jit(solution)/shard_map/all_to_all | solution.py:58
  75.9 163.5 %all-gather.9.cloned.1.call-start = ((), (), s32[]{:S(2)}) async-start(), calls=%async_computation.10 | async-start | bytes 2228224 | tf_op jit(solution)/shard_map/all_gather | solution.py:50
  118.7 1.7 copy-start.16
  119.0 1.4 copy-start.9
  123.7 7.0 %copy-start.13 = (s32[1,8,8]{2,1,0:T(8,128)S(1)}, s32[1,8,8]{2,1,0:T(8,128)}, u32[]{:S(2)}) copy-start(s32[1,8,8]{2,1,0:T(8,128)} %param.16) | copy-start | bytes 772
  123.7 7.0 %copy-start.1 = (bf16[768,16,64]{0,2,1:T(8,128)(2,1)}, bf16[768,16,64]{0,2,1:T(8,128)(2,1)S(1)}, u32[]{:S(2)}) copy-start(bf16[768,16,64]{0,2,1:T(8,128)(2,1)S(1)} %all-to-all-done) | copy-start | bytes 4718596
  123.7 115.6 %all-to-all-start.2 = ((bf16[768,16,64]{0,2,1:T(8,128)(2,1)}), bf16[768,16,64]{0,2,1:T(8,128)(2,1)}, u32[]{:S(2)}, u32[]{:S(2)}) async-start(bf16[768,16,64]{0,2,1:T(8,128)(2,1)} %bitcast.157), calls=%async_computation.2 | async-start | bytes 3145728 | tf_op jit(solution)/shard_map/all_to_all | solution.py:74
  130.7 218.8 %reduce-scatter.7.cloned.1.call-start = ((), (), s32[]{:S(2)}) async-start(), calls=%async_computation.12 | async-start | bytes 2228224 | tf_op jit(solution)/shard_map/reduce_scatter | solution.py:88
  132.4 2.9 copy-start.14
  246.6 1.1 copy-start.18
  246.6 2.6 copy-start.2
  246.9 2.1 copy-start.3
  252.6 178.3 %reduce-scatter.9.cloned.1.call-start = ((), (), s32[]{:S(2)}) async-start(), calls=%async_computation.13 | async-start | bytes 2228224 | tf_op jit(solution)/shard_map/reduce_scatter | solution.py:91
  252.9 3.3 copy-start.5
  253.2 2.1 copy-start.4
  261.3 1.6 copy-start.6
  271.3 33.8 %all-to-all-start.3 = ((bf16[768,16,64]{0,2,1:T(8,128)(2,1)}), bf16[768,16,64]{0,2,1:T(8,128)(2,1)}, u32[]{:S(2)}, u32[]{:S(2)}) async-start(bf16[768,16,64]{0,2,1:T(8,128)(2,1)} %bitcast.19), calls=%async_computation.3 | async-start | bytes 3145728 | tf_op jit(solution)/shard_map/all_to_all | solution.py:81
  284.8 28.6 %copy-start.8 = (f32[4,128,8,128]{1,0,3,2:T(4,128)S(1)}, f32[4,128,8,128]{1,0,3,2:T(4,128)}, u32[]{:S(2)}) copy-start(f32[4,128,8,128]{1,0,3,2:T(4,128)} %copy-done.7) | copy-start | bytes 6291460
  305.0 30.6 %all-to-all-start.1 = ((bf16[768,16,64]{0,2,1:T(8,128)(2,1)}), bf16[768,16,64]{0,2,1:T(8,128)(2,1)}, u32[]{:S(2)}, u32[]{:S(2)}) async-start(bf16[768,16,64]{0,2,1:T(8,128)(2,1)} %bitcast.9), calls=%async_computation.1 | async-start | bytes 3145728 | tf_op jit(solution)/shard_map/all_to_all | solution.py:63
  313.3 205.3 %reduce-scatter.13.cloned.1.call-start = ((), (), s32[]{:S(2)}) async-start(), calls=%async_computation.15 | async-start | bytes 1114112
  316.7 18.9 %copy-start.10 = (f32[8,128,4,128]{3,2,1,0:T(4,128)S(1)}, f32[8,128,4,128]{3,2,1,0:T(4,128)}, u32[]{:S(2)}) copy-start(f32[8,128,4,128]{3,2,1,0:T(4,128)} %copy-done.9) | copy-start | bytes 6291460
  319.1 287.5 %reduce-scatter.11.cloned.1.call-start = ((), (), s32[]{:S(2)}) async-start(), calls=%async_computation.14 | async-start | bytes 1114112 | tf_op jit(solution)/shard_map/reduce_scatter | solution.py:94
  340.8 1.7 copy-start.11
  342.4 3.8 copy-start.12
  342.4 3.8 copy-start.17
Sparse Core Ops, SparseCore 0:
  10.4 54.3 all-gather.4
  67.3 51.3 all-gather.10
  121.1 58.4 all-gather.6
  181.9 57.3 all-gather.8
  252.8 89.0 reduce-scatter.6
  345.7 85.1 reduce-scatter.8
  434.4 84.1 reduce-scatter.12
  522.5 84.0 reduce-scatter.10
where the time goes:
time: 617 us; the launch traced here: 615 us
  waiting for transfers between devices  481 us (78%)
  matrix products  52.8 us (9%)
  local copies, waits for them, and re-layouts  33.1 us (5%)
  starting transfers between devices  28.4 us (5%)
  between operations  14.4 us (2%)
    unnamed x9, waiting for transfers between devices  88.7 us
    reduce_scatter x1, waiting for transfers between devices, per_device(): lax.psum_scatter(term_l_down(0, hidden).astype(jnp.bfloat16), 'dp', scatt...  86.1 us
    reduce_scatter x1, waiting for transfers between devices, per_device(): lax.psum_scatter(term_r_down(0, hidden).astype(jnp.bfloat16), 'dp', scatt...  79.8 us
    all_gather x1, waiting for transfers between devices, per_device(): lax.all_gather(r_up, 'dp', axis=1, tiled=True)  54.7 us
    all_gather x1, waiting for transfers between devices, per_device(): lax.all_gather(r_down, 'dp', axis=1, tiled=True)  54.2 us
    all_gather x1, waiting for transfers between devices, per_device(): lax.all_gather(l_down, 'dp', axis=1, tiled=True)  42.2 us
    all_gather x1, waiting for transfers between devices, per_device(): lax.all_gather(l_up, 'dp', axis=1, tiled=True)  38.4 us
    all_to_all x1, waiting for transfers between devices, per_device(): lax.all_to_all(d_moved, 'tensor', split_axis=1, concat_axis=1, tiled=True)  20.3 us
  transfers between devices with their start and end apart: 12, of which 9 were waited for; matrix products, arithmetic and copies ran while one was open for 12% of the time, Pallas kernels for 0%

commit v1 on v0

v1 whole, which is shorter than its diff:
```python
import math

import jax
import jax.numpy as jnp
from jax import lax
from jax.experimental import pallas as pl
from jax.experimental.pallas import tpu as pltpu
from jax.sharding import PartitionSpec as P

MESH = pl.DeviceIdType.MESH
BF = jnp.bfloat16
F32 = jnp.float32
TOK = 768
HID = 1024
WID = 512
GELU_A = math.sqrt(2.0 / math.pi)
GELU_B = 0.044715
SCALE = 1.0 / math.sqrt(12288.0)
SHARD = ((32, 1024), (64, 1024), (64, 1024), (64, 512))


def dot(a, b, ca, cb):
    return lax.dot_general(a, b, (((ca,), (cb,)), ((), ())), preferred_element_type=F32)


def block_kernel(
    tok_hbm,
    s_r_up,
    s_l_up,
    s_r_down,
    s_l_down,
    m_r_up,
    m_l_up,
    m_r_down,
    m_l_down,
    cot_hbm,
    mixed,
    tokens_grad,
    g_r_up,
    g_l_up,
    g_r_down,
    g_l_down,
    tok,
    tok_t,
    cot,
    w_0,
    w_1,
    w_2,
    w_3,
    p_0,
    p_1,
    p_2,
    p_3,
    h_0,
    h_1,
    h_2,
    h_3,
    st_0,
    st_1,
    st_2,
    st_3,
    u_0,
    u_1,
    u_2,
    u_3,
    act,
    slope,
    d_in,
    ra_0,
    ra_1,
    ra_2,
    ra_3,
    rb_0,
    rb_1,
    rb_2,
    rb_3,
    q_0,
    q_1,
    q_2,
    q_3,
    sa_0,
    sa_1,
    sa_2,
    sa_3,
    sb_0,
    sb_1,
    sb_2,
    sb_3,
    load_sem,
    ag_send,
    ag_recv,
    a_send,
    a_recv,
    b_send,
    b_recv,
    rs_send,
    rs_recv,
):
    shards = (s_r_up, s_l_up, s_r_down, s_l_down)
    masks = (m_r_up, m_l_up, m_r_down, m_l_down)
    grads = (g_r_up, g_l_up, g_r_down, g_l_down)
    w = (w_0, w_1, w_2, w_3)
    p = (p_0, p_1, p_2, p_3)
    h = (h_0, h_1, h_2, h_3)
    st = (st_0, st_1, st_2, st_3)
    u = (u_0, u_1, u_2, u_3)
    ra = (ra_0, ra_1, ra_2, ra_3)
    rb = (rb_0, rb_1, rb_2, rb_3)
    q = (q_0, q_1, q_2, q_3)
    sa = (sa_0, sa_1, sa_2, sa_3)
    sb = (sb_0, sb_1, sb_2, sb_3)

    d = lax.axis_index("dp")
    t = lax.axis_index("tensor")
    zh, y = d // 4, d % 4
    x, j = t // 4, t % 4
    zl, c = j // 2, j % 2
    zp, zm = (zh + 1) % 4, (zh + 3) % 4
    yp, ym = (y + 1) % 4, (y + 3) % 4
    zo, yo = (zh + 2) % 4, (y + 2) % 4
    z_dev = ((zp * 4 + y, t), (zm * 4 + y, t))
    y_dev = ((zh * 4 + yp, t), (zh * 4 + ym, t))
    js = [j] + [((zl + i // 2) % 2) * 2 + (c + i % 2) % 2 for i in (1, 2, 3)]
    j_dev = [None] + [(d, x * 4 + js[i]) for i in (1, 2, 3)]
    xs = [(x + k) % 4 for k in range(4)]
    x_dev = [None] + [(d, xs[k] * 4 + j) for k in (1, 2, 3)]

    loads = [
        pltpu.make_async_copy(tok_hbm, tok, load_sem.at[0]),
        pltpu.make_async_copy(cot_hbm, cot, load_sem.at[1]),
    ]
    for copy in loads:
        copy.start()

    barrier = pltpu.get_barrier_semaphore()
    partners = list(z_dev) + list(y_dev) + j_dev[1:] + x_dev[1:]
    for device in partners:
        pl.semaphore_signal(barrier, inc=1, device_id=device, device_id_type=MESH)

    sent = []

    def remote(src, dst, send, recv, device):
        return pltpu.make_async_remote_copy(
            src_ref=src,
            dst_ref=dst,
            send_sem=send,
            recv_sem=recv,
            device_id=device,
            device_id_type=MESH,
        )

    def start(src, dst, send, recv, device):
        copy = remote(src, dst, send, recv, device)
        copy.start()
        sent.append(copy)

    def tile_row(n):
        return (d * SHARD[n][0]) // 128

    def mask_shard(n):
        rows, cols = SHARD[n]
        for tile in range(cols // 128):
            keep = masks[n][0, tile_row(n), tile].astype(F32)
            part = shards[n][0, :, tile * 128 : (tile + 1) * 128].astype(F32) * keep
            w[n][zh, pl.ds(pl.multiple_of(y * rows, rows), rows), tile * 128 : (tile + 1) * 128] = part.astype(BF)

    def at_y(ref, n, lead, which, lo=0, size=None):
        rows = SHARD[n][0]
        size = rows if size is None else size
        return ref.at[lead, pl.ds(pl.multiple_of(which * rows + lo, 16), size), :]

    def ag_places(n, stage):
        half = SHARD[n][0] // 2
        if stage == 0:
            mine = at_y(w[n], n, zh, y)
            return (mine, mine), (at_y(w[n], n, zm, y), at_y(w[n], n, zp, y))
        if stage == 1:
            return (
                (at_y(w[n], n, zm, y, 0, half), at_y(w[n], n, zp, y, half, half)),
                (at_y(w[n], n, zo, y, 0, half), at_y(w[n], n, zo, y, half, half)),
            )
        full, low, high = pl.ds(0, 4), pl.ds(0, 2), pl.ds(2, 2)
        if stage == 2:
            mine = at_y(w[n], n, full, y)
            return (mine, mine), (at_y(w[n], n, full, ym), at_y(w[n], n, full, yp))
        return (
            (at_y(w[n], n, low, ym), at_y(w[n], n, high, yp)),
            (at_y(w[n], n, low, yo), at_y(w[n], n, high, yo)),
        )

    def ag_start(n, stage):
        out, _ = ag_places(n, stage)
        devices = z_dev if stage < 2 else y_dev
        for way in (0, 1):
            start(out[way], out[way], ag_send.at[n, stage, way], ag_recv.at[n, stage, way], devices[way])

    def ag_wait(n, stage):
        _, got = ag_places(n, stage)
        devices = z_dev if stage < 2 else y_dev
        for way in (0, 1):
            remote(got[way], got[way], ag_send.at[n, stage, way], ag_recv.at[n, stage, way], devices[way]).wait_recv()

    def chunk(ref, lead, which):
        return ref.at[lead, pl.ds(pl.multiple_of(which * 64, 64), 64), :]

    def a_start(n, k):
        lead = xs[k]
        for i in (1, 2, 3):
            dst = chunk(u[n], x, j) if k == 0 else chunk(st[n], lead, j)
            start(chunk(h[n], lead, js[i]), dst, a_send.at[n, k, i - 1], a_recv.at[n, k, i - 1], j_dev[i])

    def a_wait(n, k):
        lead = xs[k]
        for i in (1, 2, 3):
            dst = chunk(u[n], x, js[i]) if k == 0 else chunk(st[n], lead, js[i])
            remote(dst, dst, a_send.at[n, k, i - 1], a_recv.at[n, k, i - 1], j_dev[i]).wait_recv()

    def own_chunks(n):
        for k in range(4):
            dst = u[n] if k == 0 else st[n]
            rows = pl.ds(pl.multiple_of(j * 64, 64), 64)
            dst[xs[k], rows, :] = h[n][xs[k], rows, :]

    def b_start(n, k):
        start(st[n].at[xs[k]], u[n].at[x], b_send.at[n, k - 1], b_recv.at[n, k - 1], x_dev[k])

    def b_wait(n, k):
        dst = u[n].at[xs[4 - k]]
        remote(dst, dst, b_send.at[n, k - 1], b_recv.at[n, k - 1], x_dev[k]).wait_recv()

    def rs_places(n, stage):
        half = SHARD[n][0] // 2
        if stage == 0:
            return (
                (at_y(p[n], n, pl.ds(0, 2), yo), at_y(p[n], n, pl.ds(2, 2), yo)),
                (ra[n].at[0, pl.ds(0, 2)], ra[n].at[1, pl.ds(0, 2)]),
            )
        if stage == 1:
            return (
                (at_y(p[n], n, pl.ds(0, 4), yp), at_y(p[n], n, pl.ds(0, 4), ym)),
                (rb[n].at[0], rb[n].at[1]),
            )
        if stage == 2:
            return (
                (q[n].at[zo, pl.ds(0, half)], q[n].at[zo, pl.ds(half, half)]),
                (sa[n].at[0], sa[n].at[1]),
            )
        return (q[n].at[zp], q[n].at[zm]), (sb[n].at[0], sb[n].at[1])

    def rs_start(n, stage):
        out, into = rs_places(n, stage)
        devices = y_dev if stage < 2 else z_dev
        for way in (0, 1):
            start(out[way], into[way], rs_send.at[n, stage, way], rs_recv.at[n, stage, way], devices[way])

    def rs_wait(n, stage):
        _, into = rs_places(n, stage)
        devices = y_dev if stage < 2 else z_dev
        for way in (0, 1):
            remote(into[way], into[way], rs_send.at[n, stage, way], rs_recv.at[n, stage, way], devices[way]).wait_recv()

    def rs_add(n, stage):
        rows, _ = SHARD[n]
        half = rows // 2

        def at(which):
            return pl.ds(pl.multiple_of(which * rows, rows), rows)

        if stage == 0:
            for way, (lead, which) in enumerate(((0, yp), (2, ym))):
                for i in (0, 1):
                    total = p[n][lead + i, at(which), :].astype(F32) + ra[n][way, i].astype(F32)
                    p[n][lead + i, at(which), :] = total.astype(BF)
        elif stage == 1:
            for i in range(4):
                total = p[n][i, at(y), :].astype(F32) + rb[n][0, i].astype(F32) + rb[n][1, i].astype(F32)
                q[n][i] = total.astype(BF)
        elif stage == 2:
            for way, (which, lo) in enumerate(((zp, 0), (zm, half))):
                total = q[n][which, lo : lo + half, :].astype(F32) + sa[n][way].astype(F32)
                q[n][which, lo : lo + half, :] = total.astype(BF)
        else:
            _, cols = SHARD[n]
            for tile in range(cols // 128):
                at_cols = slice(tile * 128, (tile + 1) * 128)
                keep = masks[n][0, tile_row(n), tile].astype(F32) * SCALE
                total = q[n][zh, :, at_cols].astype(F32) + sb[n][0, :, at_cols].astype(F32) + sb[n][1, :, at_cols].astype(F32)
                grads[n][:, at_cols] = total * keep

    def rs_step(n, stage):
        rs_wait(n, stage)
        rs_add(n, stage)
        if stage < 3:
            rs_start(n, stage + 1)

    def columns(n, k):
        part = w[n][:, :, pl.ds(pl.multiple_of(k * 256, 256), 256)]
        return part.reshape(part.shape[0] * part.shape[1], 256)

    def whole(ref):
        return ref[...].reshape(HID, ref.shape[-1])

    def each(count, step):
        lax.fori_loop(0, count, lambda k, carry: (step(k), carry)[1], 0)

    mask_shard(0)
    mask_shard(3)
    pl.semaphore_wait(barrier, len(partners))
    ag_start(0, 0)
    ag_start(3, 0)
    mask_shard(1)
    mask_shard(2)
    for copy in loads:
        copy.wait()
    tok_t[...] = tok[...].T
    for n in (0, 3):
        ag_wait(n, 0)
        ag_start(n, 1)
    ag_start(1, 0)
    ag_start(2, 0)
    for n in (0, 3):
        ag_wait(n, 1)
        ag_start(n, 2)
    for n in (1, 2):
        ag_wait(n, 0)
        ag_start(n, 1)
    for n in (0, 3):
        ag_wait(n, 2)
        ag_start(n, 3)
    for n in (1, 2):
        ag_wait(n, 1)
    ag_wait(0, 3)
    ag_start(1, 2)
    ag_start(2, 2)

    def first(k):
        h[0][k] = dot(columns(0, k), tok_t[...], 0, 0).astype(BF)

    each(4, first)
    own_chunks(0)
    a_start(0, 1)
    a_start(0, 2)
    ag_wait(3, 3)

    def back_first(k):
        h[1][k] = dot(w[3][k], cot[...], 1, 1).astype(BF)

    each(4, back_first)
    own_chunks(1)
    order = [(n, k) for n in (0, 1) for k in (1, 2, 3, 0)]

    def exchange(order, ahead, after):
        for at, (n, k) in enumerate(order):
            a_wait(n, k)
            if k:
                b_start(n, k)
            if at + ahead < len(order):
                a_start(*order[at + ahead])
            for step in after.get(at, ()):
                step()

    def more_factors():
        for n in (1, 2):
            ag_wait(n, 2)
            ag_start(n, 3)

    exchange(order, 2, {5: (more_factors,)})

    for k in (1, 2, 3):
        b_wait(0, k)
    ag_wait(1, 3)

    def inner(k):
        v = dot(columns(1, k), whole(u[0]), 0, 0)
        vv = v * v
        tanh = jnp.tanh(GELU_A * (v + GELU_B * (vv * v)))
        up = 0.5 * (1.0 + tanh)
        act[k] = (v * up).astype(BF)
        slope[k] = up + 0.5 * v * (1.0 - tanh * tanh) * (GELU_A * (1.0 + (3.0 * GELU_B) * vv))

    each(4, inner)
    ag_wait(2, 3)

    def lowered(k):
        h[2][k] = dot(columns(2, k), whole(act), 0, 0).astype(BF)

    each(4, lowered)
    own_chunks(2)
    a_start(2, 1)
    a_start(2, 2)

    for k in (1, 2, 3):
        b_wait(1, k)

    def d_inner(k):
        d_in[k] = (dot(w[2][k], whole(u[1]), 1, 0) * slope[k]).astype(BF)

    each(4, d_inner)

    def d_moved(k):
        h[3][k] = dot(w[1][k], whole(d_in), 1, 0).astype(BF)

    each(4, d_moved)
    own_chunks(3)

    def grad_r_down(k):
        p[2][k] = dot(act[k], whole(u[1]), 1, 1).astype(BF)

    def grad_l_up(k):
        p[1][k] = dot(u[0][k], whole(d_in), 1, 1).astype(BF)

    def send_r_down():
        each(4, grad_r_down)
        rs_start(2, 0)

    def send_l_up():
        each(4, grad_l_up)
        rs_start(1, 0)

    order = [(n, k) for n in (2, 3) for k in (1, 2, 3, 0)]
    exchange(
        order,
        2,
        {
            0: (send_r_down,),
            1: (send_l_up,),
            4: (lambda: rs_step(2, 0),),
            5: (lambda: rs_step(1, 0),),
        },
    )

    for k in (1, 2, 3):
        b_wait(2, k)

    def grad_l_down(k):
        p[3][k] = dot(u[2][k], cot[...], 1, 0).astype(BF)

    each(4, grad_l_down)
    rs_start(3, 0)

    def mix(k):
        cols = pl.ds(pl.multiple_of(k * 256, 256), 256)
        part = u[2][:, :, cols].reshape(HID, 256)
        mixed[cols, :] = dot(part, whole(w[3]), 0, 0).astype(BF)

    each(3, mix)
    for k in (1, 2, 3):
        b_wait(3, k)

    def grad_r_up(k):
        rows = pl.ds(pl.multiple_of(k * 128, 128), 128)
        p[0][k] = dot(tok_t[rows, :], whole(u[3]), 1, 1).astype(BF)

    each(4, grad_r_up)
    rs_start(0, 0)

    def tok_grad(k):
        part = dot(w[0][k], whole(u[3]), 1, 0)
        tokens_grad[:, pl.ds(pl.multiple_of(k * 128, 128), 128)] = part.T.astype(BF)

    each(4, tok_grad)
    rs_step(2, 1)
    rs_step(3, 0)
    rs_step(1, 1)
    rs_step(0, 0)
    rs_step(2, 2)
    rs_step(1, 2)
    rs_step(3, 1)
    rs_step(0, 1)
    rs_step(2, 3)
    rs_step(1, 3)
    rs_step(3, 2)
    rs_step(0, 2)
    rs_step(3, 3)
    rs_step(0, 3)
    for copy in sent:
        copy.wait_send()


def per_device(*args):
    vmem = pl.BlockSpec(memory_space=pltpu.VMEM)
    smem = pl.BlockSpec(memory_space=pltpu.SMEM)
    anywhere = pl.BlockSpec(memory_space=pl.ANY)
    hidden = [pltpu.VMEM((4, 256, TOK), BF)]
    full = [pltpu.VMEM((4, 4 * rows, cols), BF) for rows, cols in SHARD]
    scratch = (
        [pltpu.VMEM((TOK, WID), BF), pltpu.VMEM((WID, TOK), BF), pltpu.VMEM((TOK, WID), BF)]
        + full * 2
        + hidden * 13
        + [pltpu.VMEM((4, 256, TOK), F32)]
        + hidden
        + [pltpu.VMEM((2, 2, rows, cols), BF) for rows, cols in SHARD]
        + [pltpu.VMEM((2, 4, rows, cols), BF) for rows, cols in SHARD]
        + [pltpu.VMEM((4, rows, cols), BF) for rows, cols in SHARD]
        + [pltpu.VMEM((2, rows // 2, cols), BF) for rows, cols in SHARD]
        + [pltpu.VMEM((2, rows, cols), BF) for rows, cols in SHARD]
        + [pltpu.SemaphoreType.DMA((2,))]
        + [pltpu.SemaphoreType.DMA((4, 4, 2))] * 2
        + [pltpu.SemaphoreType.DMA((4, 4, 3))] * 2
        + [pltpu.SemaphoreType.DMA((4, 3))] * 2
        + [pltpu.SemaphoreType.DMA((4, 4, 2))] * 2
    )
    outs = pl.pallas_call(
        block_kernel,
        name="block",
        out_shape=(
            jax.ShapeDtypeStruct((TOK, WID), BF),
            jax.ShapeDtypeStruct((TOK, WID), BF),
            *(jax.ShapeDtypeStruct(shape, F32) for shape in SHARD),
        ),
        in_specs=[anywhere] + [vmem] * 4 + [smem] * 4 + [anywhere],
        out_specs=(vmem,) * 6,
        scratch_shapes=scratch,
        compiler_params=pltpu.CompilerParams(
            collective_id=0, has_side_effects=True, vmem_limit_bytes=60 * 2**20
        ),
        cost_estimate=pl.CostEstimate(
            flops=15_000_000_000, bytes_accessed=8_000_000, transcendentals=800_000
        ),
    )(*args)
    return (outs[0], outs[1], *(g[None] for g in outs[2:]))


def solution(mesh):
    weight = P("tensor", "dp", None)
    mask = P("tensor", None, None)
    act = P("dp", "tensor")
    return jax.shard_map(
        per_device,
        mesh=mesh,
        in_specs=(act, weight, weight, weight, weight, mask, mask, mask, mask, act),
        out_specs=(act, act, weight, weight, weight, weight),
        check_vma=False,
    )
```

time: 617 us -> 177 us (0.29)
  waiting for transfers between devices: 481 us -> 0 us
  Pallas kernels: 0 us -> 166 us
  matrix products: 52.8 us -> 0 us
  starting transfers between devices: 28.4 us -> 0 us
  local copies, waits for them, and re-layouts: 33.1 us -> 8.2 us
  between operations: 14.4 us -> 0.66 us
    all_gather x4 -> x0, waiting for transfers between devices: 189 us -> none  [the longest x1 54.7 us: per_device(): lax.all_gather(r_up, 'dp', axis=1, tiled=True)]
    pallas_call x0 -> x1, Pallas kernels: none -> 166 us  [per_device(): pl.pallas_call(block_kernel, name='block', out_shape=(jax.ShapeDtypeStruc...]
    reduce_scatter x3 -> x0, waiting for transfers between devices: 166 us -> none  [the longest x1 86.1 us: per_device(): lax.psum_scatter(term_l_down(0, hidden).astype(jnp.bfloat16), 'dp', scatt...]
    unnamed x9 -> x0, waiting for transfers between devices: 88.7 us -> none
    dot_general x12 -> x0, matrix products: 52.8 us -> none  [the longest x4 20.1 us: mult_back(): lax.dot_general(left, weight, (((1,), (1,)), ((), ())), preferred_element...]
    all_to_all x4 -> x0, waiting for transfers between devices: 36.7 us -> none  [the longest x1 20.3 us: per_device(): lax.all_to_all(d_moved, 'tensor', split_axis=1, concat_axis=1, tiled=True)]
    all_to_all x4 -> x0, starting transfers between devices: 27.9 us -> none  [the longest x1 8.23 us: per_device(): lax.all_to_all(lowered, 'tensor', split_axis=1, concat_axis=1, tiled=True)]
    convert_element_type x9 -> x0, local copies, waits for them, and re-layouts: 14 us -> none  [the longest x5 9.66 us: masked(): return weight[0] * spread(mask, rows, cols).astype(jnp.bfloat16)]
  transfers between devices with their start and end apart: 12 -> 0, of which waited for: 9 -> 0; matrix products, arithmetic and copies ran while one was open for 12% -> 0% of each run, Pallas kernels for 0% -> 0%
where the time goes in v1:
time: 177 us; the launch traced here: 175 us
  Pallas kernels  166 us (94%)
  local copies, waits for them, and re-layouts  8.2 us (5%)
    pallas_call x1, Pallas kernels, per_device(): pl.pallas_call(block_kernel, name='block', out_shape=(jax.ShapeDtypeStruc...  166 us
    unnamed x17, local copies, waits for them, and re-layouts  8.2 us

profile of v1, /device:TPU:32, one launch (start us, length us, event | category | flops | bytes accessed | tf_op | source)
XLA Modules:
  0.0 175.2 jit_solution(10052528865833874552)
XLA Ops:
  0.6 1.3 copy.16.m_l_down
  2.0 166.4 %block.1 = (bf16[768,512]{1,0:T(8,128)(2,1)}, bf16[768,512]{1,0:T(8,128)(2,1)}, f32[32,1024]{1,0:T(8,128)}, f32[64,1024]{1,0:T(8,128)}, f32[64,1024]{1,0:T(8,128)}, /*index=5*/f32[64,512]{1,0:T(8,128)}) custom-call(bf16[768,512]{1,0:T(8,128)(2,1)} %tok_hbm.1, bf16[1,32,1024]{2,1,0:T(8,128)(2,1)} %s_r_up.1, bf16[1,64,1024]{2,1,0:T(8,128)(2,1)} %s_l_up.1, ...), custom_call_target="tpu_custom_call" | custom-call | flops 15000000512 | bytes 8000000 | tf_op jit(solution)/shard_map/block/pallas_call | solution.py:503
  168.4 0.0 copy-start
  168.4 2.1 %copy.23 = bf16[768,512]{1,0:T(8,128)(2,1)} copy(bf16[768,512]{1,0:T(8,128)(2,1)} %get-tuple-element.24) | data formatting | bytes 1572864
  170.5 0.0 copy-done
  170.5 0.0 copy-start.4
  170.5 0.9 copy.24
  171.4 0.1 copy-done.4
  171.6 0.0 copy-start.2
  171.6 0.7 copy.25
  172.2 0.3 copy-done.2
  172.6 0.0 copy-start.1
  172.6 0.7 copy.26
  173.3 0.3 copy-done.1
  173.6 0.0 copy-start.3
  173.6 0.7 copy.27
  174.3 0.3 copy-done.3
  174.6 0.7 copy.28
Async XLA Ops:
  168.4 2.1 %copy-start = (bf16[768,512]{1,0:T(8,128)(2,1)S(1)}, bf16[768,512]{1,0:T(8,128)(2,1)}, u32[]{:S(2)}) copy-start(bf16[768,512]{1,0:T(8,128)(2,1)} %get-tuple-element.25) | copy-start | bytes 2359300
  170.5 1.0 copy-start.4
  171.6 1.0 copy-start.2
  172.6 1.0 copy-start.1
  173.6 1.0 copy-start.3

commit v2 on v1

--- a/solution.py
+++ b/solution.py
@@ -157,10 +157,15 @@
     def tile_row(n):
         return (d * SHARD[n][0]) // 128
 
+    def mask_at(n, tile):
+        if n == 3:
+            return masks[n][0, tile, tile_row(n)]
+        return masks[n][0, tile_row(n), tile]
+
     def mask_shard(n):
         rows, cols = SHARD[n]
         for tile in range(cols // 128):
-            keep = masks[n][0, tile_row(n), tile].astype(F32)
+            keep = mask_at(n, tile).astype(F32)
             part = shards[n][0, :, tile * 128 : (tile + 1) * 128].astype(F32) * keep
             w[n][zh, pl.ds(pl.multiple_of(y * rows, rows), rows), tile * 128 : (tile + 1) * 128] = part.astype(BF)
 
@@ -169,36 +174,43 @@
         size = rows if size is None else size
         return ref.at[lead, pl.ds(pl.multiple_of(which * rows + lo, 16), size), :]
 
-    def ag_places(n, stage):
+    near = (zh, zm, zp, zo)
+
+    def ag_moves(n, stage, r=0):
         half = SHARD[n][0] // 2
-        if stage == 0:
-            mine = at_y(w[n], n, zh, y)
-            return (mine, mine), (at_y(w[n], n, zm, y), at_y(w[n], n, zp, y))
-        if stage == 1:
+
+        def at(lead, which, *part):
+            return at_y(w[n], n, lead, which, *part)
+
+        if stage == "z1":
+            mine = at(zh, y)
+            return ((mine, at(zm, y), 0, z_dev[0]), (mine, at(zp, y), 1, z_dev[1]))
+        if stage == "z2":
             return (
-                (at_y(w[n], n, zm, y, 0, half), at_y(w[n], n, zp, y, half, half)),
-                (at_y(w[n], n, zo, y, 0, half), at_y(w[n], n, zo, y, half, half)),
+                (at(zm, y, 0, half), at(zo, y, 0, half), 2, z_dev[0]),
+                (at(zp, y, half, half), at(zo, y, half, half), 3, z_dev[1]),
             )
-        full, low, high = pl.ds(0, 4), pl.ds(0, 2), pl.ds(2, 2)
-        if stage == 2:
-            mine = at_y(w[n], n, full, y)
-            return (mine, mine), (at_y(w[n], n, full, ym), at_y(w[n], n, full, yp))
-        return (
-            (at_y(w[n], n, low, ym), at_y(w[n], n, high, yp)),
-            (at_y(w[n], n, low, yo), at_y(w[n], n, high, yo)),
-        )
-
-    def ag_start(n, stage):
-        out, _ = ag_places(n, stage)
-        devices = z_dev if stage < 2 else y_dev
-        for way in (0, 1):
-            start(out[way], out[way], ag_send.at[n, stage, way], ag_recv.at[n, stage, way], devices[way])
-
-    def ag_wait(n, stage):
-        _, got = ag_places(n, stage)
-        devices = z_dev if stage < 2 else y_dev
-        for way in (0, 1):
-            remote(got[way], got[way], ag_send.at[n, stage, way], ag_recv.at[n, stage, way], devices[way]).wait_recv()
+        lead = near[r]
+        if stage == "y1":
+            mine = at(lead, y)
+            return ((mine, at(lead, ym), 4 + 2 * r, y_dev[0]), (mine, at(lead, yp), 5 + 2 * r, y_dev[1]))
+        way = r % 2
+        return ((at(lead, (ym, yp)[way]), at(lead, yo), 12 + r, y_dev[way]),)
+
+    def ag_start(n, stage, *places):
+        for r in places or (0,):
+            for src, _, sem, device in ag_moves(n, stage, r):
+                start(src, src, ag_send.at[n, sem], ag_recv.at[n, sem], device)
+
+    def ag_wait(n, stage, *places):
+        for r in places or (0,):
+            for _, dst, sem, device in ag_moves(n, stage, r):
+                remote(dst, dst, ag_send.at[n, sem], ag_recv.at[n, sem], device).wait_recv()
+
+    def ag_pass(n, *places):
+        for r in places:
+            ag_wait(n, "y1", r)
+            ag_start(n, "y2", r)
 
     def chunk(ref, lead, which):
         return ref.at[lead, pl.ds(pl.multiple_of(which * 64, 64), 64), :]
@@ -283,7 +295,7 @@
             _, cols = SHARD[n]
             for tile in range(cols // 128):
                 at_cols = slice(tile * 128, (tile + 1) * 128)
-                keep = masks[n][0, tile_row(n), tile].astype(F32) * SCALE
+                keep = mask_at(n, tile).astype(F32) * SCALE
                 total = q[n][zh, :, at_cols].astype(F32) + sb[n][0, :, at_cols].astype(F32) + sb[n][1, :, at_cols].astype(F32)
                 grads[n][:, at_cols] = total * keep
 
@@ -306,69 +318,36 @@
     mask_shard(0)
     mask_shard(3)
     pl.semaphore_wait(barrier, len(partners))
-    ag_start(0, 0)
-    ag_start(3, 0)
+    for n in (0, 3):
+        ag_start(n, "z1")
+        ag_start(n, "y1", 0)
     mask_shard(1)
     mask_shard(2)
     for copy in loads:
         copy.wait()
     tok_t[...] = tok[...].T
     for n in (0, 3):
-        ag_wait(n, 0)
-        ag_start(n, 1)
-    ag_start(1, 0)
-    ag_start(2, 0)
-    for n in (0, 3):
-        ag_wait(n, 1)
-        ag_start(n, 2)
-    for n in (1, 2):
-        ag_wait(n, 0)
-        ag_start(n, 1)
-    for n in (0, 3):
-        ag_wait(n, 2)
-        ag_start(n, 3)
-    for n in (1, 2):
-        ag_wait(n, 1)
-    ag_wait(0, 3)
-    ag_start(1, 2)
-    ag_start(2, 2)
+        ag_wait(n, "z1")
+        ag_start(n, "z2")
+        ag_start(n, "y1", 1, 2)
+    ag_start(1, "z1")
+    ag_pass(0, 0)
+    ag_wait(0, "z2")
+    ag_start(0, "y1", 3)
+    ag_start(2, "z1")
+    ag_pass(0, 1, 2)
+    ag_pass(3, 0)
+    ag_wait(3, "z2")
+    ag_start(3, "y1", 3)
+    ag_pass(0, 3)
+    ag_pass(3, 1, 2)
+    ag_wait(0, "y2", 0, 1, 2, 3)
 
     def first(k):
         h[0][k] = dot(columns(0, k), tok_t[...], 0, 0).astype(BF)
 
-    each(4, first)
-    own_chunks(0)
-    a_start(0, 1)
-    a_start(0, 2)
-    ag_wait(3, 3)
-
     def back_first(k):
         h[1][k] = dot(w[3][k], cot[...], 1, 1).astype(BF)
-
-    each(4, back_first)
-    own_chunks(1)
-    order = [(n, k) for n in (0, 1) for k in (1, 2, 3, 0)]
-
-    def exchange(order, ahead, after):
-        for at, (n, k) in enumerate(order):
-            a_wait(n, k)
-            if k:
-                b_start(n, k)
-            if at + ahead < len(order):
-                a_start(*order[at + ahead])
-            for step in after.get(at, ()):
-                step()
-
-    def more_factors():
-        for n in (1, 2):
-            ag_wait(n, 2)
-            ag_start(n, 3)
-
-    exchange(order, 2, {5: (more_factors,)})
-
-    for k in (1, 2, 3):
-        b_wait(0, k)
-    ag_wait(1, 3)
 
     def inner(k):
         v = dot(columns(1, k), whole(u[0]), 0, 0)
@@ -378,103 +357,154 @@
         act[k] = (v * up).astype(BF)
         slope[k] = up + 0.5 * v * (1.0 - tanh * tanh) * (GELU_A * (1.0 + (3.0 * GELU_B) * vv))
 
-    each(4, inner)
-    ag_wait(2, 3)
-
     def lowered(k):
         h[2][k] = dot(columns(2, k), whole(act), 0, 0).astype(BF)
 
-    each(4, lowered)
-    own_chunks(2)
-    a_start(2, 1)
-    a_start(2, 2)
-
-    for k in (1, 2, 3):
-        b_wait(1, k)
-
     def d_inner(k):
         d_in[k] = (dot(w[2][k], whole(u[1]), 1, 0) * slope[k]).astype(BF)
 
-    each(4, d_inner)
-
     def d_moved(k):
         h[3][k] = dot(w[1][k], whole(d_in), 1, 0).astype(BF)
-
-    each(4, d_moved)
-    own_chunks(3)
-
-    def grad_r_down(k):
-        p[2][k] = dot(act[k], whole(u[1]), 1, 1).astype(BF)
-
-    def grad_l_up(k):
-        p[1][k] = dot(u[0][k], whole(d_in), 1, 1).astype(BF)
-
-    def send_r_down():
-        each(4, grad_r_down)
-        rs_start(2, 0)
-
-    def send_l_up():
-        each(4, grad_l_up)
-        rs_start(1, 0)
-
-    order = [(n, k) for n in (2, 3) for k in (1, 2, 3, 0)]
-    exchange(
-        order,
-        2,
-        {
-            0: (send_r_down,),
-            1: (send_l_up,),
-            4: (lambda: rs_step(2, 0),),
-            5: (lambda: rs_step(1, 0),),
-        },
-    )
-
-    for k in (1, 2, 3):
-        b_wait(2, k)
-
-    def grad_l_down(k):
-        p[3][k] = dot(u[2][k], cot[...], 1, 0).astype(BF)
-
-    each(4, grad_l_down)
-    rs_start(3, 0)
 
     def mix(k):
         cols = pl.ds(pl.multiple_of(k * 256, 256), 256)
         part = u[2][:, :, cols].reshape(HID, 256)
         mixed[cols, :] = dot(part, whole(w[3]), 0, 0).astype(BF)
 
-    each(3, mix)
-    for k in (1, 2, 3):
-        b_wait(3, k)
+    def tok_grad(k):
+        part = dot(w[0][k], whole(u[3]), 1, 0)
+        tokens_grad[:, pl.ds(pl.multiple_of(k * 128, 128), 128)] = part.T.astype(BF)
 
     def grad_r_up(k):
         rows = pl.ds(pl.multiple_of(k * 128, 128), 128)
         p[0][k] = dot(tok_t[rows, :], whole(u[3]), 1, 1).astype(BF)
 
+    def grad_l_up(k):
+        p[1][k] = dot(u[0][k], whole(d_in), 1, 1).astype(BF)
+
+    def grad_r_down(k):
+        p[2][k] = dot(act[k], whole(u[1]), 1, 1).astype(BF)
+
+    def grad_l_down(k):
+        p[3][k] = dot(u[2][k], cot[...], 1, 0).astype(BF)
+
+    def a_step(n, k):
+        a_wait(n, k)
+        if k:
+            b_start(n, k)
+
+    each(4, first)
+    own_chunks(0)
+    a_start(0, 2)
+    a_start(0, 1)
+    ag_pass(3, 3)
+    ag_wait(1, "z1")
+    ag_start(1, "z2")
+    ag_start(1, "y1", 0, 1, 2)
+    ag_wait(2, "z1")
+    ag_start(2, "z2")
+    ag_wait(3, "y2", 0, 1, 2, 3)
+    each(4, back_first)
+    own_chunks(1)
+    a_step(0, 2)
+    a_start(0, 3)
+    ag_wait(1, "z2")
+    ag_start(1, "y1", 3)
+    a_step(0, 1)
+    a_start(0, 0)
+    ag_pass(1, 0)
+    ag_wait(2, "z2")
+    ag_start(2, "y1", 0, 1, 2, 3)
+    ag_pass(1, 1, 2)
+    a_step(0, 3)
+    a_start(1, 2)
+    ag_pass(1, 3)
+    a_step(0, 0)
+    a_start(1, 1)
+    ag_pass(2, 0)
+    a_step(1, 2)
+    a_start(1, 3)
+    ag_pass(2, 1, 2)
+    a_step(1, 1)
+    a_start(1, 0)
+    ag_pass(2, 3)
+
+    for k in (2, 1, 3):
+        b_wait(0, k)
+    ag_wait(1, "y2", 0, 1, 2, 3)
+    each(4, inner)
+    a_step(1, 3)
+    ag_wait(2, "y2", 0, 1, 2, 3)
+    each(4, lowered)
+    own_chunks(2)
+    a_start(2, 2)
+    a_start(2, 1)
+    a_step(1, 0)
+    for k in (2, 1, 3):
+        b_wait(1, k)
+    each(4, grad_r_down)
+    rs_start(2, 0)
+    a_step(2, 2)
+    a_start(2, 3)
+    each(4, d_inner)
+    a_step(2, 1)
+    a_start(2, 0)
+    each(4, d_moved)
+    own_chunks(3)
+    a_start(3, 2)
+    rs_step(2, 0)
+    a_step(2, 3)
+    a_start(3, 1)
+    each(4, grad_l_up)
+    rs_start(1, 0)
+    a_step(2, 0)
+    a_start(3, 3)
+    a_step(3, 2)
+    a_start(3, 0)
+
+    for k in (2, 1, 3):
+        b_wait(2, k)
+    each(4, grad_l_down)
+    rs_start(3, 0)
+    a_step(3, 1)
+    rs_step(1, 0)
+    rs_step(2, 1)
+    a_step(3, 3)
+    each(3, mix)
+    rs_step(3, 0)
+    a_step(3, 0)
+    for k in (2, 1, 3):
+        b_wait(3, k)
     each(4, grad_r_up)
     rs_start(0, 0)
-
-    def tok_grad(k):
-        part = dot(w[0][k], whole(u[3]), 1, 0)
-        tokens_grad[:, pl.ds(pl.multiple_of(k * 128, 128), 128)] = part.T.astype(BF)
-
+    rs_step(2, 2)
     each(4, tok_grad)
-    rs_step(2, 1)
-    rs_step(3, 0)
     rs_step(1, 1)
     rs_step(0, 0)
-    rs_step(2, 2)
+    rs_step(3, 1)
     rs_step(1, 2)
-    rs_step(3, 1)
     rs_step(0, 1)
+    rs_step(3, 2)
     rs_step(2, 3)
     rs_step(1, 3)
-    rs_step(3, 2)
     rs_step(0, 2)
     rs_step(3, 3)
     rs_step(0, 3)
     for copy in sent:
         copy.wait_send()
+
+
+def write_kernel(*refs):
+    results, places, held, sem = refs[:6], refs[6:12], refs[12:18], refs[18]
+    ins = [pltpu.make_async_copy(a, b, sem.at[0, i]) for i, (a, b) in enumerate(zip(results, held))]
+    outs = [pltpu.make_async_copy(a, b, sem.at[1, i]) for i, (a, b) in enumerate(zip(held, places))]
+    for copy in ins:
+        copy.start()
+    for arrived, copy in zip(ins, outs):
+        arrived.wait()
+        copy.start()
+    for copy in outs:
+        copy.wait()
 
 
 def per_device(*args):
@@ -495,7 +525,7 @@
         + [pltpu.VMEM((2, rows // 2, cols), BF) for rows, cols in SHARD]
         + [pltpu.VMEM((2, rows, cols), BF) for rows, cols in SHARD]
         + [pltpu.SemaphoreType.DMA((2,))]
-        + [pltpu.SemaphoreType.DMA((4, 4, 2))] * 2
+        + [pltpu.SemaphoreType.DMA((4, 16))] * 2
         + [pltpu.SemaphoreType.DMA((4, 4, 3))] * 2
         + [pltpu.SemaphoreType.DMA((4, 3))] * 2
         + [pltpu.SemaphoreType.DMA((4, 4, 2))] * 2
@@ -517,7 +547,16 @@
         cost_estimate=pl.CostEstimate(
             flops=15_000_000_000, bytes_accessed=8_000_000, transcendentals=800_000
         ),
-    )(*args)
+    )(*args[:8], args[8].swapaxes(1, 2), args[9])
+    outs = pl.pallas_call(
+        write_kernel,
+        name="write",
+        out_shape=tuple(jax.ShapeDtypeStruct(o.shape, o.dtype) for o in outs),
+        in_specs=[anywhere] * 6,
+        out_specs=(anywhere,) * 6,
+        scratch_shapes=[pltpu.VMEM(o.shape, o.dtype) for o in outs] + [pltpu.SemaphoreType.DMA((2, 6))],
+        cost_estimate=pl.CostEstimate(flops=0, bytes_accessed=5_000_000, transcendentals=0),
+    )(*outs)
     return (outs[0], outs[1], *(g[None] for g in outs[2:]))
 
 

time: 177 us -> 158 us (0.89)
  Pallas kernels: 166 us -> 155 us
  local copies, waits for them, and re-layouts: 8.2 us -> 0 us
    pallas_call x1, Pallas kernels: 166 us -> 152 us  [per_device(): pl.pallas_call(block_kernel, name='block', out_shape=(jax.ShapeDtypeStruc...]
    unnamed x17 -> x0, local copies, waits for them, and re-layouts: 8.2 us -> none
    pallas_call x0 -> x1, Pallas kernels: none -> 2.63 us  [per_device(): pl.pallas_call(write_kernel, name='write', out_shape=tuple((jax.ShapeDtyp...]
where the time goes in v2:
time: 158 us; the launch traced here: 155 us
  Pallas kernels  155 us (98%)
    pallas_call x1, Pallas kernels, per_device(): pl.pallas_call(block_kernel, name='block', out_shape=(jax.ShapeDtypeStruc...  152 us

profile of v2, /device:TPU:32, one launch (start us, length us, event | category | flops | bytes accessed | tf_op | source)
XLA Modules:
  0.0 155.5 jit_solution(5939103427107103172)
XLA Ops:
  0.6 152.2 %block.1 = (bf16[768,512]{1,0:T(8,128)(2,1)}, bf16[768,512]{1,0:T(8,128)(2,1)}, f32[32,1024]{1,0:T(8,128)}, f32[64,1024]{1,0:T(8,128)}, f32[64,1024]{1,0:T(8,128)}, /*index=5*/f32[64,512]{1,0:T(8,128)}) custom-call(bf16[768,512]{1,0:T(8,128)(2,1)} %tok_hbm.1, bf16[1,32,1024]{2,1,0:T(8,128)(2,1)} %s_r_up.1, bf16[1,64,1024]{2,1,0:T(8,128)(2,1)} %s_l_up.1, ...), custom_call_target="tpu_custom_call" | custom-call | flops 15000000512 | bytes 8000000 | tf_op jit(solution)/shard_map/block/pallas_call | solution.py:533
  152.9 2.6 %write.1 = (bf16[768,512]{1,0:T(8,128)(2,1)}, bf16[768,512]{1,0:T(8,128)(2,1)}, f32[32,1024]{1,0:T(8,128)}, f32[64,1024]{1,0:T(8,128)}, f32[64,1024]{1,0:T(8,128)}, /*index=5*/f32[64,512]{1,0:T(8,128)}) custom-call(bf16[768,512]{1,0:T(8,128)(2,1)} %get-tuple-element.18.refs_0_, bf16[768,512]{1,0:T(8,128)(2,1)} %get-tuple-element.19.refs_1_, ...), custom_call_target="tpu_custom_call" | custom-call | bytes 5000000 | tf_op jit(solution)/shard_map/write/pallas_call | solution.py:551

commit v3 on v2

--- a/solution.py
+++ b/solution.py
@@ -25,21 +25,21 @@
 
 def block_kernel(
     tok_hbm,
-    s_r_up,
-    s_l_up,
-    s_r_down,
-    s_l_down,
+    r_up_hbm,
+    l_up_hbm,
+    r_down_hbm,
+    l_down_hbm,
     m_r_up,
     m_l_up,
     m_r_down,
     m_l_down,
     cot_hbm,
-    mixed,
-    tokens_grad,
-    g_r_up,
-    g_l_up,
-    g_r_down,
-    g_l_down,
+    mixed_hbm,
+    tokens_grad_hbm,
+    g_r_up_hbm,
+    g_l_up_hbm,
+    g_r_down_hbm,
+    g_l_down_hbm,
     tok,
     tok_t,
     cot,
@@ -95,6 +95,18 @@
     b_recv,
     rs_send,
     rs_recv,
+    s_r_up,
+    s_l_up,
+    s_r_down,
+    s_l_down,
+    mixed,
+    tokens_grad,
+    g_r_up,
+    g_l_up,
+    g_r_down,
+    g_l_down,
+    shard_sem,
+    out_sem,
 ):
     shards = (s_r_up, s_l_up, s_r_down, s_l_down)
     masks = (m_r_up, m_l_up, m_r_down, m_l_down)
@@ -129,13 +141,32 @@
         pltpu.make_async_copy(tok_hbm, tok, load_sem.at[0]),
         pltpu.make_async_copy(cot_hbm, cot, load_sem.at[1]),
     ]
-    for copy in loads:
-        copy.start()
+    shard_loads = [
+        pltpu.make_async_copy(src, dst, shard_sem.at[n])
+        for n, (src, dst) in enumerate(zip((r_up_hbm, l_up_hbm, r_down_hbm, l_down_hbm), shards))
+    ]
+    for n in (0, 3, 1, 2):
+        shard_loads[n].start()
+    stores = [
+        pltpu.make_async_copy(src, dst, out_sem.at[n])
+        for n, (src, dst) in enumerate(
+            (
+                (mixed, mixed_hbm),
+                (tokens_grad, tokens_grad_hbm),
+                (g_r_up, g_r_up_hbm),
+                (g_l_up, g_l_up_hbm),
+                (g_r_down, g_r_down_hbm),
+                (g_l_down, g_l_down_hbm),
+            )
+        )
+    ]
 
     barrier = pltpu.get_barrier_semaphore()
     partners = list(z_dev) + list(y_dev) + j_dev[1:] + x_dev[1:]
     for device in partners:
         pl.semaphore_signal(barrier, inc=1, device_id=device, device_id_type=MESH)
+    for copy in loads:
+        copy.start()
 
     sent = []
 
@@ -164,6 +195,7 @@
 
     def mask_shard(n):
         rows, cols = SHARD[n]
+        shard_loads[n].wait()
         for tile in range(cols // 128):
             keep = mask_at(n, tile).astype(F32)
             part = shards[n][0, :, tile * 128 : (tile + 1) * 128].astype(F32) * keep
@@ -330,15 +362,15 @@
         ag_wait(n, "z1")
         ag_start(n, "z2")
         ag_start(n, "y1", 1, 2)
-    ag_start(1, "z1")
     ag_pass(0, 0)
     ag_wait(0, "z2")
     ag_start(0, "y1", 3)
-    ag_start(2, "z1")
+    ag_start(1, "z1")
     ag_pass(0, 1, 2)
     ag_pass(3, 0)
     ag_wait(3, "z2")
     ag_start(3, "y1", 3)
+    ag_start(2, "z1")
     ag_pass(0, 3)
     ag_pass(3, 1, 2)
     ag_wait(0, "y2", 0, 1, 2, 3)
@@ -406,25 +438,27 @@
     ag_wait(3, "y2", 0, 1, 2, 3)
     each(4, back_first)
     own_chunks(1)
+    ag_pass(1, 0)
+    ag_start(2, "y1", 0)
     a_step(0, 2)
     a_start(0, 3)
     ag_wait(1, "z2")
     ag_start(1, "y1", 3)
+    ag_pass(1, 1, 2)
+    ag_start(2, "y1", 1, 2)
     a_step(0, 1)
     a_start(0, 0)
-    ag_pass(1, 0)
     ag_wait(2, "z2")
-    ag_start(2, "y1", 0, 1, 2, 3)
-    ag_pass(1, 1, 2)
+    ag_start(2, "y1", 3)
+    ag_pass(1, 3)
     a_step(0, 3)
     a_start(1, 2)
-    ag_pass(1, 3)
+    ag_pass(2, 0)
     a_step(0, 0)
     a_start(1, 1)
-    ag_pass(2, 0)
+    ag_pass(2, 1, 2)
     a_step(1, 2)
     a_start(1, 3)
-    ag_pass(2, 1, 2)
     a_step(1, 1)
     a_start(1, 0)
     ag_pass(2, 3)
@@ -471,6 +505,7 @@
     rs_step(2, 1)
     a_step(3, 3)
     each(3, mix)
+    stores[0].start()
     rs_step(3, 0)
     a_step(3, 0)
     for k in (2, 1, 3):
@@ -479,6 +514,7 @@
     rs_start(0, 0)
     rs_step(2, 2)
     each(4, tok_grad)
+    stores[1].start()
     rs_step(1, 1)
     rs_step(0, 0)
     rs_step(3, 1)
@@ -486,10 +522,16 @@
     rs_step(0, 1)
     rs_step(3, 2)
     rs_step(2, 3)
+    stores[4].start()
     rs_step(1, 3)
+    stores[3].start()
     rs_step(0, 2)
     rs_step(3, 3)
+    stores[5].start()
     rs_step(0, 3)
+    stores[2].start()
+    for copy in stores:
+        copy.wait()
     for copy in sent:
         copy.wait_send()
 
@@ -508,7 +550,6 @@
 
 
 def per_device(*args):
-    vmem = pl.BlockSpec(memory_space=pltpu.VMEM)
     smem = pl.BlockSpec(memory_space=pltpu.SMEM)
     anywhere = pl.BlockSpec(memory_space=pl.ANY)
     hidden = [pltpu.VMEM((4, 256, TOK), BF)]
@@ -529,6 +570,10 @@
         + [pltpu.SemaphoreType.DMA((4, 4, 3))] * 2
         + [pltpu.SemaphoreType.DMA((4, 3))] * 2
         + [pltpu.SemaphoreType.DMA((4, 4, 2))] * 2
+        + [pltpu.VMEM((1, rows, cols), BF) for rows, cols in SHARD]
+        + [pltpu.VMEM((TOK, WID), BF)] * 2
+        + [pltpu.VMEM(shape, F32) for shape in SHARD]
+        + [pltpu.SemaphoreType.DMA((4,)), pltpu.SemaphoreType.DMA((6,))]
     )
     outs = pl.pallas_call(
         block_kernel,
@@ -538,8 +583,8 @@
             jax.ShapeDtypeStruct((TOK, WID), BF),
             *(jax.ShapeDtypeStruct(shape, F32) for shape in SHARD),
         ),
-        in_specs=[anywhere] + [vmem] * 4 + [smem] * 4 + [anywhere],
-        out_specs=(vmem,) * 6,
+        in_specs=[anywhere] * 5 + [smem] * 4 + [anywhere],
+        out_specs=(anywhere,) * 6,
         scratch_shapes=scratch,
         compiler_params=pltpu.CompilerParams(
             collective_id=0, has_side_effects=True, vmem_limit_bytes=60 * 2**20

time: 158 us -> 157 us (level); the launches traced: 155 us -> 157 us
  no operation moved by 1% of the time
where the time goes in v3:
time: 157 us
  Pallas kernels  156 us (99%)
    pallas_call x1, Pallas kernels, per_device(): pl.pallas_call(block_kernel, name='block', out_shape=(jax.ShapeDtypeStruc...  154 us

profile of v3, /device:TPU:32, one launch (start us, length us, event | category | flops | bytes accessed | tf_op | source)
XLA Modules:
  0.0 156.9 jit_solution(15210845979455285771)
XLA Ops:
  0.6 153.6 %block.1 = (bf16[768,512]{1,0:T(8,128)(2,1)}, bf16[768,512]{1,0:T(8,128)(2,1)}, f32[32,1024]{1,0:T(8,128)}, f32[64,1024]{1,0:T(8,128)}, f32[64,1024]{1,0:T(8,128)}, /*index=5*/f32[64,512]{1,0:T(8,128)}) custom-call(bf16[768,512]{1,0:T(8,128)(2,1)} %tok_hbm.1, bf16[1,32,1024]{2,1,0:T(8,128)(2,1)} %r_up_hbm.1, bf16[1,64,1024]{2,1,0:T(8,128)(2,1)} %l_up_hbm.1, ...), custom_call_target="tpu_custom_call" | custom-call | flops 15000000512 | bytes 8000000 | tf_op jit(solution)/shard_map/block/pallas_call | solution.py:578
  154.3 2.6 %write.1 = (bf16[768,512]{1,0:T(8,128)(2,1)}, bf16[768,512]{1,0:T(8,128)(2,1)}, f32[32,1024]{1,0:T(8,128)}, f32[64,1024]{1,0:T(8,128)}, f32[64,1024]{1,0:T(8,128)}, /*index=5*/f32[64,512]{1,0:T(8,128)}) custom-call(bf16[768,512]{1,0:T(8,128)(2,1)} %get-tuple-element.18.refs_0_, bf16[768,512]{1,0:T(8,128)(2,1)} %get-tuple-element.19.refs_1_, ...), custom_call_target="tpu_custom_call" | custom-call | bytes 5000000 | tf_op jit(solution)/shard_map/write/pallas_call | solution.py:596

commit v4 on v3

--- a/solution.py
+++ b/solution.py
@@ -502,12 +502,12 @@
     rs_start(3, 0)
     a_step(3, 1)
     rs_step(1, 0)
-    rs_step(2, 1)
     a_step(3, 3)
     each(3, mix)
     stores[0].start()
     rs_step(3, 0)
     a_step(3, 0)
+    rs_step(2, 1)
     for k in (2, 1, 3):
         b_wait(3, k)
     each(4, grad_r_up)
@@ -538,8 +538,13 @@
 
 def write_kernel(*refs):
     results, places, held, sem = refs[:6], refs[6:12], refs[12:18], refs[18]
-    ins = [pltpu.make_async_copy(a, b, sem.at[0, i]) for i, (a, b) in enumerate(zip(results, held))]
-    outs = [pltpu.make_async_copy(a, b, sem.at[1, i]) for i, (a, b) in enumerate(zip(held, places))]
+    parts = []
+    for i, ref in enumerate(held):
+        rows = ref.shape[0]
+        cut = 4 if rows == TOK else 1
+        parts += [(i, pl.ds(at * (rows // cut), rows // cut)) for at in range(cut)]
+    ins = [pltpu.make_async_copy(results[i].at[at], held[i].at[at], sem.at[0, n]) for n, (i, at) in enumerate(parts)]
+    outs = [pltpu.make_async_copy(held[i].at[at], places[i].at[at], sem.at[1, n]) for n, (i, at) in enumerate(parts)]
     for copy in ins:
         copy.start()
     for arrived, copy in zip(ins, outs):
@@ -599,7 +604,7 @@
         out_shape=tuple(jax.ShapeDtypeStruct(o.shape, o.dtype) for o in outs),
         in_specs=[anywhere] * 6,
         out_specs=(anywhere,) * 6,
-        scratch_shapes=[pltpu.VMEM(o.shape, o.dtype) for o in outs] + [pltpu.SemaphoreType.DMA((2, 6))],
+        scratch_shapes=[pltpu.VMEM(o.shape, o.dtype) for o in outs] + [pltpu.SemaphoreType.DMA((2, 12))],
         cost_estimate=pl.CostEstimate(flops=0, bytes_accessed=5_000_000, transcendentals=0),
     )(*outs)
     return (outs[0], outs[1], *(g[None] for g in outs[2:]))

time: 157 us -> 157 us (level)
  no operation moved by 1% of the time
where the time goes in v4:
time: 157 us
  Pallas kernels  156 us (99%)
    pallas_call x1, Pallas kernels, per_device(): pl.pallas_call(block_kernel, name='block', out_shape=(jax.ShapeDtypeStruc...  154 us

profile of v4, /device:TPU:32, one launch (start us, length us, event | category | flops | bytes accessed | tf_op | source)
XLA Modules:
  0.0 156.9 jit_solution(5677782200905706754)
XLA Ops:
  0.6 153.6 %block.1 = (bf16[768,512]{1,0:T(8,128)(2,1)}, bf16[768,512]{1,0:T(8,128)(2,1)}, f32[32,1024]{1,0:T(8,128)}, f32[64,1024]{1,0:T(8,128)}, f32[64,1024]{1,0:T(8,128)}, /*index=5*/f32[64,512]{1,0:T(8,128)}) custom-call(bf16[768,512]{1,0:T(8,128)(2,1)} %tok_hbm.1, bf16[1,32,1024]{2,1,0:T(8,128)(2,1)} %r_up_hbm.1, bf16[1,64,1024]{2,1,0:T(8,128)(2,1)} %l_up_hbm.1, ...), custom_call_target="tpu_custom_call" | custom-call | flops 15000000512 | bytes 8000000 | tf_op jit(solution)/shard_map/block/pallas_call | solution.py:583
  154.3 2.6 %write.1 = (bf16[768,512]{1,0:T(8,128)(2,1)}, bf16[768,512]{1,0:T(8,128)(2,1)}, f32[32,1024]{1,0:T(8,128)}, f32[64,1024]{1,0:T(8,128)}, f32[64,1024]{1,0:T(8,128)}, /*index=5*/f32[64,512]{1,0:T(8,128)}) custom-call(bf16[768,512]{1,0:T(8,128)(2,1)} %get-tuple-element.18.refs_0_, bf16[768,512]{1,0:T(8,128)(2,1)} %get-tuple-element.19.refs_1_, ...), custom_call_target="tpu_custom_call" | custom-call | bytes 5000000 | tf_op jit(solution)/shard_map/write/pallas_call | solution.py:601
